TPU v7x, 1024 devices: a whole 4x4x32 slice. The times are simulated.
1024 devices in a mesh: row: 16 (over z_hi, x), col: 8 (over y, core), layer: 8 (over z_lo).
Axes of the slice: x: 4, y: 4, z: 32 (z_hi: 4, z_lo: 8; z = z_hi * 8 + z_lo), core: 2. Of those that a mesh axis runs over, the one named last changes fastest.
Arguments:
- a_tiles: bfloat16 [8, 8192, 1024], P('layer', 'row', 'col'), may hold values from -0.25 to 0.25
- b_tiles: bfloat16 [8, 1024, 16384], P('layer', 'row', 'col'), may hold values from -6 to 6
- a_mask: int32 [8, 256, 32], P('layer', 'row', 'col'), may hold values from 0 to 1
- b_mask: int32 [8, 32, 512], P('layer', 'row', 'col'), may hold values from 0 to 1
- c_mask: int32 [256, 512], P('row', 'col'), may hold values from 0 to 1
Outputs:
- product: bfloat16 [8192, 16384], P(('row', 'layer'), 'col')
All inputs are finite; a program needn't handle non-finite values.
Results may differ from a plain program's by a relative error of at most 0.001.
Values may be sent and summed in bfloat16 or wider, within the bound.
A program may use at most 64 MiB of HBM per device.

v0:
```python
import jax
import jax.numpy as jnp
from jax import lax
from jax.sharding import PartitionSpec as P

TILE = 32


def expand_tiles(values, marks):
    height, width = values.shape
    factor = marks.astype(values.dtype)
    blocks = values.reshape(height // TILE, TILE, width // TILE, TILE) * factor[:, None, :, None]
    return blocks.reshape(height, width)


def body(a_tiles, b_tiles, a_mask, b_mask, c_mask):
    left_local = expand_tiles(a_tiles[0], a_mask[0])
    right_local = expand_tiles(b_tiles[0], b_mask[0])
    a_whole = lax.all_gather(left_local, "col", axis=1, tiled=True)
    row_total = a_whole.shape[0]
    kept_mask = expand_tiles(jnp.ones((row_total, right_local.shape[1]), jnp.float32), c_mask)
    b_whole = lax.all_gather(right_local, "row", axis=0, tiled=True)
    reduced = lax.psum_scatter(
        jnp.dot(a_whole, b_whole, preferred_element_type=jnp.float32) * kept_mask,
        "layer",
        scatter_dimension=0,
        tiled=True,
    )
    return reduced.astype(jnp.bfloat16)


def solution(mesh):
    placed = (
        P("layer", "row", "col"),
        P("layer", "row", "col"),
        P("layer", "row", "col"),
        P("layer", "row", "col"),
        P("row", "col"),
    )
    return jax.shard_map(
        body, mesh=mesh, in_specs=placed, out_specs=P(("row", "layer"), "col"), check_vma=False
    )
```

profile of v0, /device:TPU:1, one launch (start us, length us, event | category | flops | bytes accessed | tf_op | source)
XLA Modules:
  0.0 434.2 jit_solution(17024003036619031657)
XLA Ops:
  6.5 0.0 copy-start
  6.5 0.0 copy-start.1
  6.5 0.0 all-gather.3.cloned.1.call-start
  6.5 0.7 convert_bitcast_fusion
  7.3 0.1 copy.7
  7.4 0.2 mul.30
  7.6 0.3 mul.31
  7.9 1.6 bitcast_multiply_fusion.1
  9.5 0.0 all-gather.3.cloned.1.call-update
  9.5 0.0 all-gather.5.cloned.1.call-start
  9.5 0.7 convert_bitcast_fusion.1
  10.2 0.3 mul.33
  10.5 1.2 mul.34
  11.7 0.0 copy-done
  11.7 0.7 bitcast_multiply_fusion
  12.5 0.0 all-gather.5.cloned.1.call-update
  12.5 0.0 reduce-scatter.2.cloned.1.call-start
  12.5 0.0 copy-done.1
  12.5 7.9 %mul.36 = f32[16,32,64,32]{3,2,1,0:T(8,128)} broadcast(f32[16,64]{1,0:T(8,128)S(1)} %convert_element_type.30), dimensions={0,2} | broadcast | bytes 4198400 | tf_op jit(solution)/shard_map/mul | solution.py:12
  20.5 13.4 %reshape.22 = f32[512,2048]{1,0:T(8,128)} reshape(f32[16,32,64,32]{3,2,1,0:T(8,128)} %mul.36) | data formatting | bytes 8388608 | tf_op jit(solution)/shard_map/reshape | solution.py:13
  33.9 26.2 %all-gather.3.cloned.1.call-done = bf16[512,1024]{1,0:T(8,128)(2,1)} async-done(((bf16[512,128]{1,0:T(8,128)(2,1)}), bf16[512,1024]{1,0:T(8,128)(2,1)}) %all-gather.3.cloned.1.call-update) | async-done | bytes 1048592 | tf_op jit(solution)/shard_map/all_gather | solution.py:19
  60.1 254.4 %all-gather.5.cloned.1.call-done = bf16[1024,2048]{1,0:T(8,128)(2,1)} async-done(((bf16[64,2048]{1,0:T(8,128)(2,1)}), bf16[1024,2048]{1,0:T(8,128)(2,1)}) %all-gather.5.cloned.1.call-update) | async-done | bytes 4194320 | tf_op jit(solution)/shard_map/all_gather | solution.py:22
  314.6 8.1 %convolution_multiply_fusion = f32[512,2048]{1,0:T(8,128)} fusion(f32[512,2048]{1,0:T(8,128)} %reshape.22, bf16[512,1024]{1,0:T(8,128)(2,1)} %all-gather.3.cloned.1.call-done, bf16[1024,2048]{1,0:T(8,128)(2,1)} %all-gather.5.cloned.1.call-done), kind=kOutput, calls=%fused_computation | convolution fusion | flops 2148532224 | bytes 13631488 | tf_op jit(solution)/shard_map/dot_general | solution.py:24
  322.7 0.0 reduce-scatter.2.cloned.1.call-update
  322.7 103.2 %reduce-scatter.2.cloned.1.call-done = f32[64,2048]{1,0:T(8,128)} async-done(((f32[512,2048]{1,0:T(8,128)}), f32[64,2048]{1,0:T(8,128)}) %reduce-scatter.2.cloned.1.call-update) | async-done | bytes 524304 | tf_op jit(solution)/shard_map/reduce_scatter | solution.py:23
  425.9 1.8 convert_element_type.31
  (1 shorter events, 0.0 us)
Async XLA Ops:
  6.5 5.2 %copy-start = (bf16[1,64,2048]{2,1,0:T(8,128)(2,1)S(1)}, bf16[1,64,2048]{2,1,0:T(8,128)(2,1)}, u32[]{:S(2)}) copy-start(bf16[1,64,2048]{2,1,0:T(8,128)(2,1)} %param.6) | copy-start | bytes 786436
  6.5 6.0 %copy-start.1 = (s32[16,64]{1,0:T(8,128)S(1)}, s32[16,64]{1,0:T(8,128)}, u32[]{:S(2)}) copy-start(s32[16,64]{1,0:T(8,128)} %param.9) | copy-start | bytes 12292
  6.5 53.6 %all-gather.3.cloned.1.call-start = ((), (), s32[]{:S(2)}) async-start(), calls=%async_computation.1 | async-start | bytes 1179648 | tf_op jit(solution)/shard_map/all_gather | solution.py:19
  9.5 305.1 %all-gather.5.cloned.1.call-start = ((), (), s32[]{:S(2)}) async-start(), calls=%async_computation.2 | async-start | bytes 4456448 | tf_op jit(solution)/shard_map/all_gather | solution.py:22
  12.5 413.4 %reduce-scatter.2.cloned.1.call-start = ((), (), s32[]{:S(2)}) async-start(), calls=%async_computation.3 | async-start | bytes 4718592 | tf_op jit(solution)/shard_map/reduce_scatter | solution.py:23
Sparse Core Ops, SparseCore 0:
  10.1 50.0 all-gather.2
  64.3 250.2 all-gather.4
  322.8 103.0 reduce-scatter.1
where the time goes:
time: 435 us; the launch traced here: 434 us
  waiting for transfers between devices  384 us (88%)
  local copies, waits for them, and re-layouts  23.5 us (5%)
  between operations  13.2 us (3%)
  matrix products  8.09 us (2%)
  other arithmetic  5.51 us (1%)
    all_gather x1, waiting for transfers between devices, body(): b_whole = lax.all_gather(right_local, 'row', axis=0, tiled=True)  254 us
    reduce_scatter x1, waiting for transfers between devices, body(): lax.psum_scatter(jnp.dot(a_whole, b_whole, preferred_element_type=jnp.flo...  103 us
    all_gather x1, waiting for transfers between devices, body(): a_whole = lax.all_gather(left_local, 'col', axis=1, tiled=True)  26.2 us
    reshape x1, local copies, waits for them, and re-layouts, expand_tiles(): return blocks.reshape(height, width)  13.4 us
    mul x5, local copies, waits for them, and re-layouts, expand_tiles(): values.reshape(height // TILE, TILE, width // TILE, TILE)  9.91 us
  transfers between devices with their start and end apart: 3, of which 3 were waited for; matrix products, arithmetic and copies ran while one was open for 6% of the time, Pallas kernels for 0%

commit v1 on v0

v1 whole, which is shorter than its diff:
```python
import jax
import jax.numpy as jnp
from jax import lax
from jax.experimental import pallas as pl
from jax.experimental.pallas import tpu as pltpu
from jax.sharding import PartitionSpec as P

TILE = 32
RUN = 8
RING = 32
SIDE = 4
WIDE = 256
DEEP = 64
ROWS = 512
NARROW = 128
MESH = pl.DeviceIdType.MESH
F32 = jnp.float32
BF16 = jnp.bfloat16


def device(x, y, z, core):
    return ((z // RUN) * SIDE + x, y * 2 + core, z % RUN)


def piece_of(z):
    low = z % RUN
    return jnp.where((z // RUN) % 2 == 0, low, RUN - 1 - low)


def frame_of(source, piece):
    m = jnp.where(piece < RUN // 2, piece, RUN - 1 - piece)
    turn = jnp.where(piece < RUN // 2, 0, RUN)
    ahead = lax.rem(source - turn - m + 2 * RING, RING)
    start = lax.rem(turn + 16 * (ahead // 16), RING)
    return m, start, m + lax.rem(ahead, 16)


def spread_rows(factor):
    height, width = factor.shape
    return jnp.broadcast_to(factor[:, None, :], (height, TILE, width)).reshape(height * TILE, width)


def kernel(
    a_ref, b_ref, a_mask_ref, b_mask_ref, c_mask_ref, o_ref,
    left, right, own, total, done, landed,
    b_send, b_pass, b_recv, x_send, x_recv, a_send, a_recv, y_send, y_recv, k_send, k_recv, c_send, c_recv,
):
    row, col, zl = lax.axis_index("row"), lax.axis_index("col"), lax.axis_index("layer")
    x, zh = lax.rem(row, SIDE), row // SIDE
    y, core = col // 2, lax.rem(col, 2)
    z = zh * RUN + zl
    mine = piece_of(z)

    def at_z(there):
        return device(x, y, lax.rem(there + RING, RING), core)

    def at_x(step):
        return device(lax.rem(x + step, SIDE), y, z, core)

    def at_y(step):
        return device(x, lax.rem(y + step, SIDE), z, core)

    other = device(x, y, z, 1 - core)

    barrier = pltpu.get_barrier_semaphore()

    @pl.loop(1, RING)
    def _(step):
        pl.semaphore_signal(barrier, inc=1, device_id=at_z(z + step), device_id_type=MESH)

    for step in range(1, SIDE):
        pl.semaphore_signal(barrier, inc=1, device_id=at_x(step), device_id_type=MESH)
        pl.semaphore_signal(barrier, inc=1, device_id=at_y(step), device_id_type=MESH)
    pl.semaphore_signal(barrier, inc=1, device_id=other, device_id_type=MESH)

    marks = a_mask_ref[...].astype(F32)
    lane = lax.broadcasted_iota(jnp.int32, (ROWS // TILE, NARROW), 1) // TILE
    factor = jnp.zeros((ROWS // TILE, NARROW), F32)
    for tile in range(NARROW // TILE):
        factor = jnp.where(lane == tile, marks[:, tile : tile + 1], factor)
    left[zl, core, y] = (a_ref[...].astype(F32) * spread_rows(factor)).astype(BF16)

    width = b_ref.shape[1]
    tiles = width // TILE
    marks = b_mask_ref[...].astype(F32)
    spread = (
        lax.broadcasted_iota(jnp.int32, (tiles, width), 0) == lax.broadcasted_iota(jnp.int32, (tiles, width), 1) // TILE
    ).astype(F32)
    factor = spread_rows(jnp.dot(marks, spread, preferred_element_type=F32))
    for piece in range(RUN):
        cut = slice(piece * WIDE, (piece + 1) * WIDE)
        own[piece] = (b_ref[:, cut].astype(F32) * factor[:, cut]).astype(BF16)
    right[zl, zh, x] = own[mine]

    pl.semaphore_wait(barrier, RING - 1 + 2 * (SIDE - 1) + 1)

    def a_hop(low, to):
        return pltpu.make_async_remote_copy(
            src_ref=left.at[low, core, y], dst_ref=left.at[low, core, y],
            send_sem=a_send.at[low, jnp.where(to > zl, 1, 0)], recv_sem=a_recv.at[low],
            device_id=device(x, y, zh * RUN + to, core), device_id_type=MESH,
        )

    def a_side(low, step):
        return pltpu.make_async_remote_copy(
            src_ref=left.at[low, core, y], dst_ref=left.at[low, core, y],
            send_sem=y_send.at[low, step - 1], recv_sem=y_recv.at[low],
            device_id=at_y(step), device_id_type=MESH,
        )

    def a_core(low):
        return pltpu.make_async_remote_copy(
            src_ref=left.at[low, core], dst_ref=left.at[low, core],
            send_sem=k_send.at[low], recv_sem=k_recv.at[low],
            device_id=other, device_id_type=MESH,
        )

    def a_onward(low):
        @pl.when((low <= zl) & (zl < RUN - 1))
        def _():
            a_hop(low, zl + 1).start()

        @pl.when((low >= zl) & (zl > 0))
        def _():
            a_hop(low, zl - 1).start()

        for step in (1, 3, 2):
            a_side(low, step).start()

    def a_arrive(low):
        pltpu.make_async_copy(left.at[low, core, y], left.at[low, core, y], a_recv.at[low]).wait()
        a_onward(low)

    def a_share(low):
        view = left.at[low, core, pl.ds(0, SIDE - 1)]
        pltpu.make_async_copy(view, view, y_recv.at[low]).wait()
        a_core(low).start()

    def both_ways(step, act):
        @pl.when(zl - step >= 0)
        def _():
            act(zl - step)

        @pl.when(zl + step < RUN)
        def _():
            act(zl + step)

    def b_first(piece, to, way):
        return pltpu.make_async_remote_copy(
            src_ref=own.at[piece], dst_ref=right.at[zl, zh, x],
            send_sem=b_send.at[piece, way], recv_sem=b_recv.at[z],
            device_id=at_z(to), device_id_type=MESH,
        )

    def b_next(source, to):
        low, high = lax.rem(source, RUN), source // RUN
        return pltpu.make_async_remote_copy(
            src_ref=right.at[low, high, x], dst_ref=right.at[low, high, x],
            send_sem=b_pass.at[source], recv_sem=b_recv.at[source],
            device_id=at_z(to), device_id_type=MESH,
        )

    def b_side(source, step):
        low, high = lax.rem(source, RUN), source // RUN
        return pltpu.make_async_remote_copy(
            src_ref=right.at[low, high, x], dst_ref=right.at[low, high, x],
            send_sem=x_send.at[source, step - 1], recv_sem=x_recv.at[source],
            device_id=at_x(step), device_id_type=MESH,
        )

    def first_of(piece):
        m, start, at = frame_of(z, piece)
        inside = at <= 15 - m
        up = jnp.where(inside, 15 - m, 16 + m)
        down = jnp.where(inside, m, 15 - m)
        return lax.rem(start + up, RING), at != up, lax.rem(start + down, RING), at != down

    def route(source):
        m, start, at = frame_of(source, mine)
        here = lax.rem(z - start + RING, RING)
        inside = at <= 15 - m
        odd = lax.rem(source + mine, 2) == 1
        t0, t1, t2, t3 = m, 15 - m, 16 + m, 31 - m
        is0, is1, is2, is3 = here == t0, here == t1, here == t2, here == t3
        hops_in = jnp.where(is0 | is1, 1, 2)
        to_in = jnp.where(is0, t3, jnp.where(is1, t2, -1))
        hops_up = jnp.where(is1 | is2, 1, jnp.where(is3, 2, 3))
        to_up = jnp.where(is2, t3, jnp.where(is3, t0, -1))
        hops_down = jnp.where(is1 | is2, 1, jnp.where(is0, 2, 3))
        to_down = jnp.where(is1, t0, jnp.where(is0, t3, -1))
        hops = jnp.where(inside, hops_in, jnp.where(odd, hops_up, hops_down))
        to = jnp.where(inside, to_in, jnp.where(odd, to_up, to_down))
        return hops, to >= 0, lax.rem(start + to + RING, RING)

    def b_handle(source, hops_now):
        hops, onward, to = route(source)

        @pl.when(hops == hops_now)
        def _():
            low, high = lax.rem(source, RUN), source // RUN

            @pl.when(source != z)
            def _():
                pltpu.make_async_copy(right.at[low, high, x], right.at[low, high, x], b_recv.at[source]).wait()

            @pl.when(onward)
            def _():
                b_next(source, to).start()

            for step in (1, 3, 2):
                b_side(source, step).start()

    def source_at(index):
        away = (index + 1) // 2
        return lax.rem(z + jnp.where(lax.rem(index, 2) == 0, away, RING - away), RING)

    a_onward(zl)

    @pl.loop(0, RUN)
    def _(step):
        piece = lax.rem(mine + step, RUN)
        to_up, up, to_down, down = first_of(piece)

        @pl.when(up)
        def _():
            b_first(piece, to_up, 1).start()

        @pl.when(down)
        def _():
            b_first(piece, to_down, 0).start()

    @pl.loop(0, RUN)
    def _(step):
        @pl.loop(0, RING // RUN)
        def _(index):
            b_handle(source_at(step * (RING // RUN) + index), 1)

        both_ways(step + 1, a_arrive)

    a_share(zl)

    @pl.loop(0, RUN)
    def _(step):
        @pl.loop(0, RING // RUN)
        def _(index):
            b_handle(source_at(step * (RING // RUN) + index), 2)

        both_ways(step + 1, a_share)

    @pl.loop(0, RING)
    def _(index):
        b_handle(source_at(index), 3)

    total[...] = jnp.zeros_like(total)

    @pl.loop(0, RUN)
    def _(low):
        pltpu.make_async_copy(left.at[low, core], left.at[low, core], k_recv.at[low]).wait()
        for high in range(RING // RUN):
            view = right.at[low, high, pl.ds(0, SIDE - 1)]
            pltpu.make_async_copy(view, view, x_recv.at[high * RUN + low]).wait()
        blocks = [left[low, c, s] for s in range(SIDE) for c in range(2)]
        total[...] += jnp.dot(
            jnp.concatenate(blocks, axis=1),
            right[low].reshape(RING // RUN * SIDE * DEEP, WIDE),
            preferred_element_type=F32,
        )

    keep = (
        lax.broadcasted_iota(jnp.int32, (tiles, WIDE), 0)
        == lax.broadcasted_iota(jnp.int32, (tiles, WIDE), 1) // TILE + mine * (WIDE // TILE)
    ).astype(F32)
    factor = jnp.dot(c_mask_ref[...].astype(F32), keep, preferred_element_type=F32)
    done[...] = (total[...] * spread_rows(factor)).astype(BF16).reshape(RUN, ROWS // RUN, WIDE)
    landed[mine] = done[zl]

    def c_out(low):
        return pltpu.make_async_remote_copy(
            src_ref=done.at[low], dst_ref=landed.at[mine],
            send_sem=c_send.at[low], recv_sem=c_recv,
            device_id=device(x, y, zh * RUN + low, core), device_id_type=MESH,
        )

    @pl.loop(1, RUN)
    def _(step):
        c_out(lax.rem(zl + step, RUN)).start()

    view = landed.at[pl.ds(0, RUN - 1)]
    pltpu.make_async_copy(view, view, c_recv).wait()
    for piece in range(RUN):
        o_ref[:, piece * WIDE : (piece + 1) * WIDE] = landed[piece]

    @pl.loop(0, RUN)
    def _(index):
        @pl.when((index <= zl) & (zl < RUN - 1))
        def _():
            a_hop(index, zl + 1).wait_send()

        @pl.when((index >= zl) & (zl > 0))
        def _():
            a_hop(index, zl - 1).wait_send()

        for step in (1, 2, 3):
            a_side(index, step).wait_send()
        a_core(index).wait_send()

        to_up, up, to_down, down = first_of(index)

        @pl.when(up)
        def _():
            b_first(index, to_up, 1).wait_send()

        @pl.when(down)
        def _():
            b_first(index, to_down, 0).wait_send()

        @pl.when(index != zl)
        def _():
            c_out(index).wait_send()

    @pl.loop(0, RING)
    def _(source):
        _, onward, to = route(source)

        @pl.when(onward)
        def _():
            b_next(source, to).wait_send()

        for step in (1, 2, 3):
            b_side(source, step).wait_send()


def body(a_tiles, b_tiles, a_mask, b_mask, c_mask):
    width = b_tiles.shape[2]
    dma = pltpu.SemaphoreType.DMA
    return pl.pallas_call(
        kernel,
        out_shape=jax.ShapeDtypeStruct((ROWS // RUN, width), BF16),
        in_specs=[pl.BlockSpec(memory_space=pltpu.VMEM)] * 5,
        out_specs=pl.BlockSpec(memory_space=pltpu.VMEM),
        scratch_shapes=[
            pltpu.VMEM((RUN, 2, SIDE, ROWS, NARROW), BF16),
            pltpu.VMEM((RUN, RING // RUN, SIDE, DEEP, WIDE), BF16),
            pltpu.VMEM((RUN, DEEP, WIDE), BF16),
            pltpu.VMEM((ROWS, WIDE), F32),
            pltpu.VMEM((RUN, ROWS // RUN, WIDE), BF16),
            pltpu.VMEM((RUN, ROWS // RUN, WIDE), BF16),
            dma((RUN, 2)), dma((RING,)), dma((RING,)),
            dma((RING, SIDE - 1)), dma((RING,)),
            dma((RUN, 2)), dma((RUN,)),
            dma((RUN, SIDE - 1)), dma((RUN,)),
            dma((RUN,)), dma((RUN,)),
            dma((RUN,)), dma,
        ],
        compiler_params=pltpu.CompilerParams(
            collective_id=0, has_side_effects=True, vmem_limit_bytes=40 << 20
        ),
        cost_estimate=pl.CostEstimate(
            flops=2 * ROWS * WIDE * 8192, bytes_accessed=1 << 20, transcendentals=0
        ),
        name="purify",
    )(a_tiles[0], b_tiles[0], a_mask[0], b_mask[0], c_mask)


def solution(mesh):
    placed = (
        P("layer", "row", "col"),
        P("layer", "row", "col"),
        P("layer", "row", "col"),
        P("layer", "row", "col"),
        P("row", "col"),
    )
    return jax.shard_map(
        body, mesh=mesh, in_specs=placed, out_specs=P(("row", "layer"), "col"), check_vma=False
    )
```

time: 435 us -> 155 us (0.36)
  the two profiles are of different devices: /device:TPU:1 before, /device:TPU:16 now
where the time goes in v1:
time: 155 us
  Pallas kernels  151 us (97%)
  local copies, waits for them, and re-layouts  3.92 us (3%)
    pallas_call x1, Pallas kernels, body(): pl.pallas_call(kernel, out_shape=jax.ShapeDtypeStruct((ROWS // RUN, width...  151 us
    unnamed x11, local copies, waits for them, and re-layouts  3.83 us

profile of v1, /device:TPU:16, one launch (start us, length us, event | category | flops | bytes accessed | tf_op | source)
XLA Modules:
  0.0 155.1 jit_solution(11527364902093400825)
XLA Ops:
  0.0 0.0 copy-start.4
  0.0 0.0 copy-start.2
  0.0 0.7 copy-done.4
  0.7 0.0 copy-start.3
  0.7 0.1 copy.6.a_mask_ref
  0.8 0.0 copy-done.2
  0.8 0.6 copy-done.3
  1.4 0.0 copy-start
  1.4 0.9 copy-done
  2.3 0.0 copy-start.1
  2.3 0.9 copy-done.1
  3.2 151.2 %purify.1 = bf16[64,2048]{1,0:T(8,128)(2,1)S(1)} custom-call(bf16[512,128]{1,0:T(8,128)(2,1)S(1)} %bitcast.5, bf16[64,2048]{1,0:T(8,128)(2,1)S(1)} %bitcast.4, s32[16,4]{1,0:T(8,128)S(1)} %copy.6.a_mask_ref, s32[2,64]{1,0:T(2,128)S(1)} %bitcast.6, s32[16,64]{1,0:T(8,128)S(1)} %copy-done.2), custom_call_target="tpu_custom_call" | custom-call | flops 2147483648 | bytes 1048576 | tf_op jit(solution)/shard_map/purify/pallas_call | solution.py:336
  154.4 0.7 copy.8
Async XLA Ops:
  0.0 0.7 copy-start.4
  0.0 0.8 copy-start.2
  0.7 0.7 copy-start.3
  1.4 0.9 copy-start
  2.3 0.9 copy-start.1

commit v2 on v1

v2 whole, which is shorter than its diff:
```python
import jax
import jax.numpy as jnp
from jax import lax
from jax.experimental import pallas as pl
from jax.experimental.pallas import tpu as pltpu
from jax.sharding import PartitionSpec as P

TILE = 32
RUN = 8
RING = 32
SIDE = 4
WIDE = 256
DEEP = 64
ROWS = 512
NARROW = 128
HALVES = 1
HALF = WIDE // HALVES
GPS = 2
LAG2 = 3
LAG3 = 4
MESH = pl.DeviceIdType.MESH
F32 = jnp.float32
BF16 = jnp.bfloat16


def device(x, y, z, core):
    return (lax.div(z, RUN) * SIDE + x, y * 2 + core, lax.rem(z, RUN))


def wrap(number, size):
    return jnp.where(number >= size, number - size, number)


def mirrored(index, high):
    return jnp.where(high % 2 == 0, index, RUN - 1 - index)


def lap_of(source, piece):
    early = piece < RUN // 2
    m = jnp.where(early, piece, RUN - 1 - piece)
    ahead = source - jnp.where(early, m, m + RUN)
    ahead = jnp.where(ahead < 0, ahead + RING, ahead)
    far = ahead >= 16
    return 15 - 2 * m, jnp.where(far, ahead - 16, ahead), far


def spread_rows(factor):
    height, width = factor.shape
    return jnp.broadcast_to(factor[:, None, :], (height, TILE, width)).reshape(height * TILE, width)


def kernel(
    a_ref, b_ref, a_mask_ref, b_mask_ref, c_mask_ref, o_ref,
    a_in, b_in, left, right, own, total, done, landed,
    in_sem, b_send, b_pass, b_recv, x_send, x_recv, a_send, a_recv, y_send, y_recv, k_send, k_recv, c_send, c_recv,
):
    row, col, zl = lax.axis_index("row"), lax.axis_index("col"), lax.axis_index("layer")
    x, zh = lax.rem(row, SIDE), row // SIDE
    y, core = col // 2, lax.rem(col, 2)
    z = zh * RUN + zl
    mine = mirrored(zl, zh)

    a_copy = pltpu.make_async_copy(a_ref, a_in, in_sem.at[0])
    b_copy = pltpu.make_async_copy(b_ref, b_in, in_sem.at[1])
    a_copy.start()
    b_copy.start()

    def at_z(there):
        return device(x, y, there, core)

    def at_x(step):
        return device(wrap(x + step, SIDE), y, z, core)

    def at_y(step):
        return device(x, wrap(y + step, SIDE), z, core)

    other = device(x, y, z, 1 - core)

    barrier = pltpu.get_barrier_semaphore()

    for high in range(RING // RUN):
        for low in range(RUN):
            @pl.when((zl != low) | (zh != high))
            def _():
                pl.semaphore_signal(barrier, inc=1, device_id=(high * SIDE + x, col, low), device_id_type=MESH)

    for step in range(1, SIDE):
        pl.semaphore_signal(barrier, inc=1, device_id=at_x(step), device_id_type=MESH)
        pl.semaphore_signal(barrier, inc=1, device_id=at_y(step), device_id_type=MESH)
    pl.semaphore_signal(barrier, inc=1, device_id=other, device_id_type=MESH)

    marks = a_mask_ref[...].astype(F32)
    lane = lax.broadcasted_iota(jnp.int32, (ROWS // TILE, NARROW), 1) // TILE
    factor = jnp.zeros((ROWS // TILE, NARROW), F32)
    for tile in range(NARROW // TILE):
        factor = jnp.where(lane == tile, marks[:, tile : tile + 1], factor)
    a_copy.wait()
    left[zl, core, y] = (a_in[...].astype(F32) * spread_rows(factor)).astype(BF16)

    width = b_ref.shape[1]
    tiles = width // TILE
    marks = b_mask_ref[...].astype(F32)
    spread = (
        lax.broadcasted_iota(jnp.int32, (tiles, width), 0) == lax.broadcasted_iota(jnp.int32, (tiles, width), 1) // TILE
    ).astype(F32)
    factor = spread_rows(jnp.dot(marks, spread, preferred_element_type=F32))
    b_copy.wait()
    for piece in range(RUN):
        for half in range(HALVES):
            cut = slice(piece * WIDE + half * HALF, piece * WIDE + (half + 1) * HALF)
            own[half, piece] = (b_in[:, cut].astype(F32) * factor[:, cut]).astype(BF16)
    for half in range(HALVES):
        right[half, mine, x, zh] = own[half, mine]

    pl.semaphore_wait(barrier, RING - 1 + 2 * (SIDE - 1) + 1)

    def a_hop(low, to):
        return pltpu.make_async_remote_copy(
            src_ref=left.at[low, core, y], dst_ref=left.at[low, core, y],
            send_sem=a_send.at[low, jnp.where(to > zl, 1, 0)], recv_sem=a_recv.at[low],
            device_id=device(x, y, zh * RUN + to, core), device_id_type=MESH,
        )

    def a_side(low, step):
        return pltpu.make_async_remote_copy(
            src_ref=left.at[low, core, y], dst_ref=left.at[low, core, y],
            send_sem=y_send.at[low, step - 1], recv_sem=y_recv.at[low],
            device_id=at_y(step), device_id_type=MESH,
        )

    def a_core(low):
        return pltpu.make_async_remote_copy(
            src_ref=left.at[low, core], dst_ref=left.at[low, core],
            send_sem=k_send.at[low], recv_sem=k_recv.at[low],
            device_id=other, device_id_type=MESH,
        )

    def a_onward(low):
        @pl.when((low <= zl) & (zl < RUN - 1))
        def _():
            a_hop(low, zl + 1).start()

        @pl.when((low >= zl) & (zl > 0))
        def _():
            a_hop(low, zl - 1).start()

        for step in (1, 3, 2):
            a_side(low, step).start()

    def a_arrive(low):
        pltpu.make_async_copy(left.at[low, core, y], left.at[low, core, y], a_recv.at[low]).wait()
        a_onward(low)

    def a_share(low):
        view = left.at[low, core, pl.ds(0, SIDE - 1)]
        pltpu.make_async_copy(view, view, y_recv.at[low]).wait()
        a_core(low).start()

    def both_ways(step, act):
        @pl.when(zl - step >= 0)
        def _():
            act(zl - step)

        @pl.when(zl + step < RUN)
        def _():
            act(zl + step)

    def b_first(half, piece, to, way):
        return pltpu.make_async_remote_copy(
            src_ref=own.at[half, piece], dst_ref=right.at[half, mine, x, zh],
            send_sem=b_send.at[half, piece, way], recv_sem=b_recv.at[half, mine, zh],
            device_id=at_z(to), device_id_type=MESH,
        )

    def b_next(half, index, high, to):
        return pltpu.make_async_remote_copy(
            src_ref=right.at[half, index, x, high], dst_ref=right.at[half, index, x, high],
            send_sem=b_pass.at[half, index, high], recv_sem=b_recv.at[half, index, high],
            device_id=at_z(to), device_id_type=MESH,
        )

    def b_side(half, index, high, step):
        return pltpu.make_async_remote_copy(
            src_ref=right.at[half, index, x, high], dst_ref=right.at[half, index, x, high],
            send_sem=x_send.at[half, index, high, step - 1], recv_sem=x_recv.at[half, index],
            device_id=at_x(step), device_id_type=MESH,
        )

    def first_of(piece):
        gap, behind, _ = lap_of(z, piece)
        inside = behind <= gap
        up = jnp.where(inside, gap, 16) - behind
        down = behind - jnp.where(inside, 0, gap)
        return wrap(z + up, RING), up > 0, wrap(z - down + RING, RING), down > 0

    wide, behind_me, far_me = lap_of(z, mine)
    role = jnp.where(behind_me == 0, 0, 1) + jnp.where(far_me, 2, 0)
    narrow = 16 - wide

    def part(role):
        inside = jnp.where(role < 2, 1, 2), jnp.where(role == 0, -narrow, jnp.where(role == 1, narrow, 0))
        middle = (role == 1) | (role == 2)
        odd = (
            jnp.where(middle, 1, jnp.where(role == 3, 2, 3)),
            jnp.where(role == 2, wide, jnp.where(role == 3, narrow, 0)),
        )
        even = (
            jnp.where(middle, 1, jnp.where(role == 0, 2, 3)),
            jnp.where(role == 1, -wide, jnp.where(role == 0, -narrow, 0)),
        )
        return [64 * hops + 32 + step for hops, step in (inside, odd, even)]

    near_parts = part(role)
    far_parts = part(wrap(role + 2, 4))

    def route(index, high):
        low = mirrored(index, high)
        _, behind, far = lap_of(high * RUN + low, mine)
        near_code = jnp.where(behind <= wide, near_parts[0], jnp.where(lax.rem(low + mine, 2) == 1, near_parts[1], near_parts[2]))
        far_code = jnp.where(behind <= wide, far_parts[0], jnp.where(lax.rem(low + mine, 2) == 1, far_parts[1], far_parts[2]))
        code = jnp.where(far, far_code, near_code)
        step = lax.rem(code, 64) - 32
        return lax.div(code, 64), step != 0, lax.rem(z + step + RING, RING)

    def group_of(stage):
        half = stage // RUN
        return half, wrap(mine - (stage - half * RUN) + RUN, RUN)

    def b_launch(stage):
        half = stage // RUN
        piece = wrap(mine + stage - half * RUN, RUN)
        to_up, up, to_down, down = first_of(piece)

        @pl.when(up)
        def _():
            b_first(half, piece, to_up, 1).start()

        @pl.when(down)
        def _():
            b_first(half, piece, to_down, 0).start()

    def b_handle(stage, hops_now):
        half, index = group_of(stage)
        for high in range(RING // RUN):
            hops, onward, to = route(index, high)

            @pl.when(hops == hops_now)
            def _():
                @pl.when((index != mine) | (high != zh))
                def _():
                    view = right.at[half, index, x, high]
                    pltpu.make_async_copy(view, view, b_recv.at[half, index, high]).wait()

                @pl.when(onward)
                def _():
                    b_next(half, index, high, to).start()

                for side in (1, 3, 2):
                    b_side(half, index, high, side).start()

    def use(stage):
        half, index = group_of(stage)
        view = right.at[half, index, pl.ds(0, SIDE - 1)]
        pltpu.make_async_copy(view, view, x_recv.at[half, index]).wait()
        lows = [index if high % 2 == 0 else RUN - 1 - index for high in range(RING // RUN)]
        blocks = [left[lows[high], c, high] for high in range(SIDE) for c in range(2)]
        depths = [right[half, index, s, high] for high in range(RING // RUN) for s in range(SIDE)]
        total[half] += jnp.dot(
            jnp.concatenate(blocks, axis=1), jnp.concatenate(depths, axis=0), preferred_element_type=F32
        )

    def c_out(half, low):
        return pltpu.make_async_remote_copy(
            src_ref=done.at[half, low], dst_ref=landed.at[half, mine],
            send_sem=c_send.at[half, low], recv_sem=c_recv.at[half],
            device_id=device(x, y, zh * RUN + low, core), device_id_type=MESH,
        )

    def finish(half):
        keep = (
            lax.broadcasted_iota(jnp.int32, (tiles, HALF), 0)
            == lax.broadcasted_iota(jnp.int32, (tiles, HALF), 1) // TILE + mine * (WIDE // TILE) + half * (HALF // TILE)
        ).astype(F32)
        factor = jnp.dot(c_mask_ref[...].astype(F32), keep, preferred_element_type=F32)
        done[half] = (total[half] * spread_rows(factor)).astype(BF16).reshape(RUN, ROWS // RUN, HALF)

        @pl.loop(1, RUN)
        def _(step):
            c_out(half, wrap(zl + step, RUN)).start()

        landed[half, mine] = done[half, zl]

    a_onward(zl)
    total[...] = jnp.zeros_like(total)

    @pl.loop(0, RUN)
    def _(stage):
        b_launch(stage)

    last = max(RUN + 1, RUN // GPS + LAG3)

    def staged(step, act):
        for turn in range(GPS):
            stage = step * GPS + turn

            @pl.when((stage >= 0) & (stage < RUN))
            def _():
                act(stage)

    @pl.loop(0, last)
    def _(step):
        @pl.when(step < RUN - 1)
        def _():
            both_ways(step + 1, a_arrive)

        staged(step, lambda stage: b_handle(stage, 1))
        staged(step - LAG2, lambda stage: b_handle(stage, 2))
        staged(step - LAG3, lambda stage: b_handle(stage, 3))

        @pl.when((step >= 1) & (step < RUN + 1))
        def _():
            @pl.when(step == 1)
            def _():
                a_share(zl)

            @pl.when(step > 1)
            def _():
                both_ways(step - 1, a_share)

    @pl.loop(0, RUN)
    def _(low):
        pltpu.make_async_copy(left.at[low, core], left.at[low, core], k_recv.at[low]).wait()

    @pl.loop(0, RUN)
    def _(stage):
        use(stage)

    finish(HALVES - 1)

    @pl.loop(0, RUN)
    def _(index):
        @pl.when((index <= zl) & (zl < RUN - 1))
        def _():
            a_hop(index, zl + 1).wait_send()

        @pl.when((index >= zl) & (zl > 0))
        def _():
            a_hop(index, zl - 1).wait_send()

        for step in (1, 2, 3):
            a_side(index, step).wait_send()
        a_core(index).wait_send()

        to_up, up, to_down, down = first_of(index)
        for half in range(HALVES):
            @pl.when(up)
            def _():
                b_first(half, index, to_up, 1).wait_send()

            @pl.when(down)
            def _():
                b_first(half, index, to_down, 0).wait_send()

            for high in range(RING // RUN):
                for step in (1, 2, 3):
                    b_side(half, index, high, step).wait_send()

        for high in range(RING // RUN):
            _, onward, to = route(index, high)

            @pl.when(onward)
            def _():
                for half in range(HALVES):
                    b_next(half, index, high, to).wait_send()

    for half in range(HALVES):
        view = landed.at[half, pl.ds(0, RUN - 1)]
        pltpu.make_async_copy(view, view, c_recv.at[half]).wait()
        for piece in range(RUN):
            cut = slice(piece * WIDE + half * HALF, piece * WIDE + (half + 1) * HALF)
            o_ref[:, cut] = landed[half, piece]

    @pl.loop(0, RUN)
    def _(index):
        @pl.when(index != zl)
        def _():
            for half in range(HALVES):
                c_out(half, index).wait_send()


def body(a_tiles, b_tiles, a_mask, b_mask, c_mask):
    width = b_tiles.shape[2]
    dma = pltpu.SemaphoreType.DMA
    runs = RING // RUN
    return pl.pallas_call(
        kernel,
        out_shape=jax.ShapeDtypeStruct((ROWS // RUN, width), BF16),
        in_specs=[pl.BlockSpec(memory_space=pltpu.HBM)] * 2 + [pl.BlockSpec(memory_space=pltpu.VMEM)] * 3,
        out_specs=pl.BlockSpec(memory_space=pltpu.VMEM),
        scratch_shapes=[
            pltpu.VMEM((ROWS, NARROW), BF16),
            pltpu.VMEM((DEEP, width), BF16),
            pltpu.VMEM((RUN, 2, SIDE, ROWS, NARROW), BF16),
            pltpu.VMEM((HALVES, RUN, SIDE, runs, DEEP, HALF), BF16),
            pltpu.VMEM((HALVES, RUN, DEEP, HALF), BF16),
            pltpu.VMEM((HALVES, ROWS, HALF), F32),
            pltpu.VMEM((HALVES, RUN, ROWS // RUN, HALF), BF16),
            pltpu.VMEM((HALVES, RUN, ROWS // RUN, HALF), BF16),
            dma((2,)),
            dma((HALVES, RUN, 2)), dma((HALVES, RUN, runs)), dma((HALVES, RUN, runs)),
            dma((HALVES, RUN, runs, SIDE - 1)), dma((HALVES, RUN)),
            dma((RUN, 2)), dma((RUN,)),
            dma((RUN, SIDE - 1)), dma((RUN,)),
            dma((RUN,)), dma((RUN,)),
            dma((HALVES, RUN)), dma((HALVES,)),
        ],
        compiler_params=pltpu.CompilerParams(
            collective_id=0, has_side_effects=True, vmem_limit_bytes=63 << 20
        ),
        cost_estimate=pl.CostEstimate(
            flops=2 * ROWS * WIDE * 8192, bytes_accessed=1 << 20, transcendentals=0
        ),
        name="purify",
    )(a_tiles[0], b_tiles[0], a_mask[0], b_mask[0], c_mask)


def solution(mesh):
    placed = (
        P("layer", "row", "col"),
        P("layer", "row", "col"),
        P("layer", "row", "col"),
        P("layer", "row", "col"),
        P("row", "col"),
    )
    return jax.shard_map(
        body, mesh=mesh, in_specs=placed, out_specs=P(("row", "layer"), "col"), check_vma=False
    )
```

time: 155 us -> 141 us (0.910)
  the two profiles are of different devices: /device:TPU:16 before, /device:TPU:1 now
where the time goes in v2:
time: 141 us
  Pallas kernels  138 us (98%)
  local copies, waits for them, and re-layouts  3.03 us (2%)
    pallas_call x1, Pallas kernels, body(): pl.pallas_call(kernel, out_shape=jax.ShapeDtypeStruct((ROWS // RUN, width...  138 us

profile of v2, /device:TPU:1, one launch (start us, length us, event | category | flops | bytes accessed | tf_op | source)
XLA Modules:
  0.0 141.1 jit_solution(5129805386112182749)
XLA Ops:
  0.0 0.0 copy-start
  0.0 0.7 copy-done
  0.7 0.7 copy.6.a_mask_ref
  1.4 138.1 %purify.1 = bf16[64,2048]{1,0:T(8,128)(2,1)} custom-call(bf16[512,128]{1,0:T(8,128)(2,1)} %bitcast.6, bf16[64,2048]{1,0:T(8,128)(2,1)} %bitcast.5, s32[16,4]{1,0:T(8,128)} %copy.6.a_mask_ref, s32[2,64]{1,0:T(2,128)} %bitcast.7, s32[16,64]{1,0:T(8,128)} %c_mask_ref.1), custom_call_target="tpu_custom_call" | custom-call | flops 2147483648 | bytes 1048576 | tf_op jit(solution)/shard_map/purify/pallas_call | solution.py:395
  139.4 1.7 %copy.8 = bf16[64,2048]{1,0:T(8,128)(2,1)} copy(bf16[64,2048]{1,0:T(8,128)(2,1)} %purify.1) | data formatting | bytes 524288
Async XLA Ops:
  0.0 0.7 copy-start

commit v3 on v2

--- a/solution.py
+++ b/solution.py
@@ -51,8 +51,8 @@
 
 def kernel(
     a_ref, b_ref, a_mask_ref, b_mask_ref, c_mask_ref, o_ref,
-    a_in, b_in, left, right, own, total, done, landed,
-    in_sem, b_send, b_pass, b_recv, x_send, x_recv, a_send, a_recv, y_send, y_recv, k_send, k_recv, c_send, c_recv,
+    a_in, b_in, a_marks, b_marks, c_marks, left, right, own, total, done, landed,
+    in_sem, b_send, b_pass, b_recv, x_send, x_recv, a_send, a_recv, y_send, y_near, y_recv, k_send, k_recv, c_send, c_recv,
 ):
     row, col, zl = lax.axis_index("row"), lax.axis_index("col"), lax.axis_index("layer")
     x, zh = lax.rem(row, SIDE), row // SIDE
@@ -62,8 +62,14 @@
 
     a_copy = pltpu.make_async_copy(a_ref, a_in, in_sem.at[0])
     b_copy = pltpu.make_async_copy(b_ref, b_in, in_sem.at[1])
-    a_copy.start()
-    b_copy.start()
+    mask_copies = [
+        pltpu.make_async_copy(source, held, in_sem.at[2 + number])
+        for number, (source, held) in enumerate(
+            ((a_mask_ref, a_marks), (b_mask_ref, b_marks), (c_mask_ref, c_marks))
+        )
+    ]
+    for copy in (mask_copies[0], a_copy, mask_copies[1], b_copy, mask_copies[2]):
+        copy.start()
 
     def at_z(there):
         return device(x, y, there, core)
@@ -89,17 +95,21 @@
         pl.semaphore_signal(barrier, inc=1, device_id=at_y(step), device_id_type=MESH)
     pl.semaphore_signal(barrier, inc=1, device_id=other, device_id_type=MESH)
 
-    marks = a_mask_ref[...].astype(F32)
-    lane = lax.broadcasted_iota(jnp.int32, (ROWS // TILE, NARROW), 1) // TILE
-    factor = jnp.zeros((ROWS // TILE, NARROW), F32)
-    for tile in range(NARROW // TILE):
-        factor = jnp.where(lane == tile, marks[:, tile : tile + 1], factor)
+    mask_copies[0].wait()
+    spread = (
+        lax.broadcasted_iota(jnp.int32, (NARROW // TILE, NARROW), 0)
+        == lax.broadcasted_iota(jnp.int32, (NARROW // TILE, NARROW), 1) // TILE
+    ).astype(F32)
+    factor = lax.dot_general(
+        a_marks[...].astype(F32), spread, (((0,), (0,)), ((), ())), preferred_element_type=F32
+    )
     a_copy.wait()
     left[zl, core, y] = (a_in[...].astype(F32) * spread_rows(factor)).astype(BF16)
 
     width = b_ref.shape[1]
     tiles = width // TILE
-    marks = b_mask_ref[...].astype(F32)
+    mask_copies[1].wait()
+    marks = b_marks[...].astype(F32)
     spread = (
         lax.broadcasted_iota(jnp.int32, (tiles, width), 0) == lax.broadcasted_iota(jnp.int32, (tiles, width), 1) // TILE
     ).astype(F32)
@@ -121,12 +131,22 @@
             device_id=device(x, y, zh * RUN + to, core), device_id_type=MESH,
         )
 
-    def a_side(low, step):
-        return pltpu.make_async_remote_copy(
-            src_ref=left.at[low, core, y], dst_ref=left.at[low, core, y],
-            send_sem=y_send.at[low, step - 1], recv_sem=y_recv.at[low],
+    way = jnp.where(core == 0, 1, SIDE - 1)
+    back = SIDE - way
+
+    def a_side(low, whose, step, near):
+        there = wrap(y + whose, SIDE)
+        return pltpu.make_async_remote_copy(
+            src_ref=left.at[low, core, there], dst_ref=left.at[low, core, there],
+            send_sem=y_send.at[low, 0 if near else jnp.where(whose == 0, 1, 2)],
+            recv_sem=y_near.at[low] if near else y_recv.at[low],
             device_id=at_y(step), device_id_type=MESH,
         )
+
+    def a_relay(low):
+        view = left.at[low, core, wrap(y + back, SIDE)]
+        pltpu.make_async_copy(view, view, y_near.at[low]).wait()
+        a_side(low, back, way, False).start()
 
     def a_core(low):
         return pltpu.make_async_remote_copy(
@@ -144,15 +164,15 @@
         def _():
             a_hop(low, zl - 1).start()
 
-        for step in (1, 3, 2):
-            a_side(low, step).start()
+        a_side(low, 0, way, True).start()
+        a_side(low, 0, back, False).start()
 
     def a_arrive(low):
         pltpu.make_async_copy(left.at[low, core, y], left.at[low, core, y], a_recv.at[low]).wait()
         a_onward(low)
 
     def a_share(low):
-        view = left.at[low, core, pl.ds(0, SIDE - 1)]
+        view = left.at[low, core, pl.ds(0, 2)]
         pltpu.make_async_copy(view, view, y_recv.at[low]).wait()
         a_core(low).start()
 
@@ -281,7 +301,7 @@
             lax.broadcasted_iota(jnp.int32, (tiles, HALF), 0)
             == lax.broadcasted_iota(jnp.int32, (tiles, HALF), 1) // TILE + mine * (WIDE // TILE) + half * (HALF // TILE)
         ).astype(F32)
-        factor = jnp.dot(c_mask_ref[...].astype(F32), keep, preferred_element_type=F32)
+        factor = jnp.dot(c_marks[...].astype(F32), keep, preferred_element_type=F32)
         done[half] = (total[half] * spread_rows(factor)).astype(BF16).reshape(RUN, ROWS // RUN, HALF)
 
         @pl.loop(1, RUN)
@@ -292,6 +312,7 @@
 
     a_onward(zl)
     total[...] = jnp.zeros_like(total)
+    mask_copies[2].wait()
 
     @pl.loop(0, RUN)
     def _(stage):
@@ -313,6 +334,14 @@
         def _():
             both_ways(step + 1, a_arrive)
 
+        @pl.when(step == 0)
+        def _():
+            a_relay(zl)
+
+        @pl.when((step > 0) & (step < RUN))
+        def _():
+            both_ways(step, a_relay)
+
         staged(step, lambda stage: b_handle(stage, 1))
         staged(step - LAG2, lambda stage: b_handle(stage, 2))
         staged(step - LAG3, lambda stage: b_handle(stage, 3))
@@ -347,8 +376,9 @@
         def _():
             a_hop(index, zl - 1).wait_send()
 
-        for step in (1, 2, 3):
-            a_side(index, step).wait_send()
+        a_side(index, 0, way, True).wait_send()
+        a_side(index, 0, back, False).wait_send()
+        a_side(index, back, way, False).wait_send()
         a_core(index).wait_send()
 
         to_up, up, to_down, down = first_of(index)
@@ -395,22 +425,25 @@
     return pl.pallas_call(
         kernel,
         out_shape=jax.ShapeDtypeStruct((ROWS // RUN, width), BF16),
-        in_specs=[pl.BlockSpec(memory_space=pltpu.HBM)] * 2 + [pl.BlockSpec(memory_space=pltpu.VMEM)] * 3,
+        in_specs=[pl.BlockSpec(memory_space=pltpu.HBM)] * 5,
         out_specs=pl.BlockSpec(memory_space=pltpu.VMEM),
         scratch_shapes=[
             pltpu.VMEM((ROWS, NARROW), BF16),
             pltpu.VMEM((DEEP, width), BF16),
+            pltpu.VMEM((NARROW // TILE, ROWS // TILE), jnp.int32),
+            pltpu.VMEM((DEEP // TILE, width // TILE), jnp.int32),
+            pltpu.VMEM((ROWS // TILE, width // TILE), jnp.int32),
             pltpu.VMEM((RUN, 2, SIDE, ROWS, NARROW), BF16),
             pltpu.VMEM((HALVES, RUN, SIDE, runs, DEEP, HALF), BF16),
             pltpu.VMEM((HALVES, RUN, DEEP, HALF), BF16),
             pltpu.VMEM((HALVES, ROWS, HALF), F32),
             pltpu.VMEM((HALVES, RUN, ROWS // RUN, HALF), BF16),
             pltpu.VMEM((HALVES, RUN, ROWS // RUN, HALF), BF16),
-            dma((2,)),
+            dma((5,)),
             dma((HALVES, RUN, 2)), dma((HALVES, RUN, runs)), dma((HALVES, RUN, runs)),
             dma((HALVES, RUN, runs, SIDE - 1)), dma((HALVES, RUN)),
             dma((RUN, 2)), dma((RUN,)),
-            dma((RUN, SIDE - 1)), dma((RUN,)),
+            dma((RUN, SIDE - 1)), dma((RUN,)), dma((RUN,)),
             dma((RUN,)), dma((RUN,)),
             dma((HALVES, RUN)), dma((HALVES,)),
         ],
@@ -421,7 +454,7 @@
             flops=2 * ROWS * WIDE * 8192, bytes_accessed=1 << 20, transcendentals=0
         ),
         name="purify",
-    )(a_tiles[0], b_tiles[0], a_mask[0], b_mask[0], c_mask)
+    )(a_tiles[0], b_tiles[0], a_mask[0].T, b_mask[0], c_mask)
 
 
 def solution(mesh):

time: 141 us -> 139 us (0.986)
  no operation moved by 1% of the time
where the time goes in v3:
time: 139 us
  Pallas kernels  138 us (99%)
  local copies, waits for them, and re-layouts  1.67 us (1%)
    pallas_call x1, Pallas kernels, body(): pl.pallas_call(kernel, out_shape=jax.ShapeDtypeStruct((ROWS // RUN, width...  138 us

profile of v3, /device:TPU:1, one launch (start us, length us, event | category | flops | bytes accessed | tf_op | source)
XLA Modules:
  0.0 139.3 jit_solution(11302675804992608064)
XLA Ops:
  0.0 137.6 %purify.1 = bf16[64,2048]{1,0:T(8,128)(2,1)} custom-call(bf16[512,128]{1,0:T(8,128)(2,1)} %bitcast.7, bf16[64,2048]{1,0:T(8,128)(2,1)} %bitcast.6, s32[4,16]{1,0:T(4,128)} %bitcast.8, s32[2,64]{1,0:T(2,128)} %bitcast.9, s32[16,64]{1,0:T(8,128)} %c_mask_ref.1), custom_call_target="tpu_custom_call" | custom-call | flops 2147483648 | bytes 1048576 | tf_op jit(solution)/shard_map/purify/pallas_call | solution.py:425
  137.6 1.7 %copy.7 = bf16[64,2048]{1,0:T(8,128)(2,1)} copy(bf16[64,2048]{1,0:T(8,128)(2,1)} %purify.1) | data formatting | bytes 524288

commit v4 on v3

--- a/solution.py
+++ b/solution.py
@@ -106,6 +106,196 @@
     a_copy.wait()
     left[zl, core, y] = (a_in[...].astype(F32) * spread_rows(factor)).astype(BF16)
 
+    pl.semaphore_wait(barrier, RING - 1 + 2 * (SIDE - 1) + 1)
+
+    def a_hop(low, to):
+        return pltpu.make_async_remote_copy(
+            src_ref=left.at[low, core, y], dst_ref=left.at[low, core, y],
+            send_sem=a_send.at[low, jnp.where(to > zl, 1, 0)], recv_sem=a_recv.at[low],
+            device_id=device(x, y, zh * RUN + to, core), device_id_type=MESH,
+        )
+
+    way = jnp.where(core == 0, 1, SIDE - 1)
+    back = SIDE - way
+
+    def a_side(low, whose, step, near):
+        there = wrap(y + whose, SIDE)
+        return pltpu.make_async_remote_copy(
+            src_ref=left.at[low, core, there], dst_ref=left.at[low, core, there],
+            send_sem=y_send.at[low, 0 if near else jnp.where(whose == 0, 1, 2)],
+            recv_sem=y_near.at[low] if near else y_recv.at[low],
+            device_id=at_y(step), device_id_type=MESH,
+        )
+
+    def a_relay(low):
+        view = left.at[low, core, wrap(y + back, SIDE)]
+        pltpu.make_async_copy(view, view, y_near.at[low]).wait()
+        a_side(low, back, way, False).start()
+
+    def a_core(low):
+        return pltpu.make_async_remote_copy(
+            src_ref=left.at[low, core], dst_ref=left.at[low, core],
+            send_sem=k_send.at[low], recv_sem=k_recv.at[low],
+            device_id=other, device_id_type=MESH,
+        )
+
+    def a_onward(low):
+        @pl.when((low <= zl) & (zl < RUN - 1))
+        def _():
+            a_hop(low, zl + 1).start()
+
+        @pl.when((low >= zl) & (zl > 0))
+        def _():
+            a_hop(low, zl - 1).start()
+
+        a_side(low, 0, way, True).start()
+        a_side(low, 0, back, False).start()
+
+    def a_arrive(low):
+        pltpu.make_async_copy(left.at[low, core, y], left.at[low, core, y], a_recv.at[low]).wait()
+        a_onward(low)
+
+    def a_share(low):
+        view = left.at[low, core, pl.ds(0, 2)]
+        pltpu.make_async_copy(view, view, y_recv.at[low]).wait()
+        a_core(low).start()
+
+    def both_ways(step, act):
+        @pl.when(zl - step >= 0)
+        def _():
+            act(zl - step)
+
+        @pl.when(zl + step < RUN)
+        def _():
+            act(zl + step)
+
+    def b_first(half, piece, to, way):
+        return pltpu.make_async_remote_copy(
+            src_ref=own.at[half, piece], dst_ref=right.at[half, mine, x, zh],
+            send_sem=b_send.at[half, piece, way], recv_sem=b_recv.at[half, mine, zh],
+            device_id=at_z(to), device_id_type=MESH,
+        )
+
+    def b_next(half, index, high, to):
+        return pltpu.make_async_remote_copy(
+            src_ref=right.at[half, index, x, high], dst_ref=right.at[half, index, x, high],
+            send_sem=b_pass.at[half, index, high], recv_sem=b_recv.at[half, index, high],
+            device_id=at_z(to), device_id_type=MESH,
+        )
+
+    def b_side(half, index, high, step):
+        return pltpu.make_async_remote_copy(
+            src_ref=right.at[half, index, x, high], dst_ref=right.at[half, index, x, high],
+            send_sem=x_send.at[half, index, high, step - 1], recv_sem=x_recv.at[half, index],
+            device_id=at_x(step), device_id_type=MESH,
+        )
+
+    def first_of(piece):
+        gap, behind, _ = lap_of(z, piece)
+        inside = behind <= gap
+        up = jnp.where(inside, gap, 16) - behind
+        down = behind - jnp.where(inside, 0, gap)
+        return wrap(z + up, RING), up > 0, wrap(z - down + RING, RING), down > 0
+
+    wide, behind_me, far_me = lap_of(z, mine)
+    role = jnp.where(behind_me == 0, 0, 1) + jnp.where(far_me, 2, 0)
+    narrow = 16 - wide
+
+    def part(role):
+        inside = jnp.where(role < 2, 1, 2), jnp.where(role == 0, -narrow, jnp.where(role == 1, narrow, 0))
+        middle = (role == 1) | (role == 2)
+        odd = (
+            jnp.where(middle, 1, jnp.where(role == 3, 2, 3)),
+            jnp.where(role == 2, wide, jnp.where(role == 3, narrow, 0)),
+        )
+        even = (
+            jnp.where(middle, 1, jnp.where(role == 0, 2, 3)),
+            jnp.where(role == 1, -wide, jnp.where(role == 0, -narrow, 0)),
+        )
+        return [64 * hops + 32 + step for hops, step in (inside, odd, even)]
+
+    near_parts = part(role)
+    far_parts = part(wrap(role + 2, 4))
+
+    def route(index, high):
+        low = mirrored(index, high)
+        _, behind, far = lap_of(high * RUN + low, mine)
+        near_code = jnp.where(behind <= wide, near_parts[0], jnp.where(lax.rem(low + mine, 2) == 1, near_parts[1], near_parts[2]))
+        far_code = jnp.where(behind <= wide, far_parts[0], jnp.where(lax.rem(low + mine, 2) == 1, far_parts[1], far_parts[2]))
+        code = jnp.where(far, far_code, near_code)
+        step = lax.rem(code, 64) - 32
+        return lax.div(code, 64), step != 0, lax.rem(z + step + RING, RING)
+
+    def group_of(stage):
+        half = stage // RUN
+        return half, wrap(mine - (stage - half * RUN) + RUN, RUN)
+
+    def b_launch(stage):
+        half = stage // RUN
+        piece = wrap(mine + stage - half * RUN, RUN)
+        to_up, up, to_down, down = first_of(piece)
+
+        @pl.when(up)
+        def _():
+            b_first(half, piece, to_up, 1).start()
+
+        @pl.when(down)
+        def _():
+            b_first(half, piece, to_down, 0).start()
+
+    def b_handle(stage, hops_now):
+        half, index = group_of(stage)
+        for high in range(RING // RUN):
+            hops, onward, to = route(index, high)
+
+            @pl.when(hops == hops_now)
+            def _():
+                @pl.when((index != mine) | (high != zh))
+                def _():
+                    view = right.at[half, index, x, high]
+                    pltpu.make_async_copy(view, view, b_recv.at[half, index, high]).wait()
+
+                @pl.when(onward)
+                def _():
+                    b_next(half, index, high, to).start()
+
+                for side in (1, 3, 2):
+                    b_side(half, index, high, side).start()
+
+    def use(stage):
+        half, index = group_of(stage)
+        view = right.at[half, index, pl.ds(0, SIDE - 1)]
+        pltpu.make_async_copy(view, view, x_recv.at[half, index]).wait()
+        lows = [index if high % 2 == 0 else RUN - 1 - index for high in range(RING // RUN)]
+        blocks = [left[lows[high], c, high] for high in range(SIDE) for c in range(2)]
+        depths = [right[half, index, s, high] for high in range(RING // RUN) for s in range(SIDE)]
+        total[half] += jnp.dot(
+            jnp.concatenate(blocks, axis=1), jnp.concatenate(depths, axis=0), preferred_element_type=F32
+        )
+
+    def c_out(half, low):
+        return pltpu.make_async_remote_copy(
+            src_ref=done.at[half, low], dst_ref=landed.at[half, mine],
+            send_sem=c_send.at[half, low], recv_sem=c_recv.at[half],
+            device_id=device(x, y, zh * RUN + low, core), device_id_type=MESH,
+        )
+
+    def finish(half):
+        keep = (
+            lax.broadcasted_iota(jnp.int32, (tiles, HALF), 0)
+            == lax.broadcasted_iota(jnp.int32, (tiles, HALF), 1) // TILE + mine * (WIDE // TILE) + half * (HALF // TILE)
+        ).astype(F32)
+        factor = jnp.dot(c_marks[...].astype(F32), keep, preferred_element_type=F32)
+        done[half] = (total[half] * spread_rows(factor)).astype(BF16).reshape(RUN, ROWS // RUN, HALF)
+
+        @pl.loop(1, RUN)
+        def _(step):
+            c_out(half, wrap(zl + step, RUN)).start()
+
+        landed[half, mine] = done[half, zl]
+
+    a_onward(zl)
+
     width = b_ref.shape[1]
     tiles = width // TILE
     mask_copies[1].wait()
@@ -121,196 +311,6 @@
             own[half, piece] = (b_in[:, cut].astype(F32) * factor[:, cut]).astype(BF16)
     for half in range(HALVES):
         right[half, mine, x, zh] = own[half, mine]
-
-    pl.semaphore_wait(barrier, RING - 1 + 2 * (SIDE - 1) + 1)
-
-    def a_hop(low, to):
-        return pltpu.make_async_remote_copy(
-            src_ref=left.at[low, core, y], dst_ref=left.at[low, core, y],
-            send_sem=a_send.at[low, jnp.where(to > zl, 1, 0)], recv_sem=a_recv.at[low],
-            device_id=device(x, y, zh * RUN + to, core), device_id_type=MESH,
-        )
-
-    way = jnp.where(core == 0, 1, SIDE - 1)
-    back = SIDE - way
-
-    def a_side(low, whose, step, near):
-        there = wrap(y + whose, SIDE)
-        return pltpu.make_async_remote_copy(
-            src_ref=left.at[low, core, there], dst_ref=left.at[low, core, there],
-            send_sem=y_send.at[low, 0 if near else jnp.where(whose == 0, 1, 2)],
-            recv_sem=y_near.at[low] if near else y_recv.at[low],
-            device_id=at_y(step), device_id_type=MESH,
-        )
-
-    def a_relay(low):
-        view = left.at[low, core, wrap(y + back, SIDE)]
-        pltpu.make_async_copy(view, view, y_near.at[low]).wait()
-        a_side(low, back, way, False).start()
-
-    def a_core(low):
-        return pltpu.make_async_remote_copy(
-            src_ref=left.at[low, core], dst_ref=left.at[low, core],
-            send_sem=k_send.at[low], recv_sem=k_recv.at[low],
-            device_id=other, device_id_type=MESH,
-        )
-
-    def a_onward(low):
-        @pl.when((low <= zl) & (zl < RUN - 1))
-        def _():
-            a_hop(low, zl + 1).start()
-
-        @pl.when((low >= zl) & (zl > 0))
-        def _():
-            a_hop(low, zl - 1).start()
-
-        a_side(low, 0, way, True).start()
-        a_side(low, 0, back, False).start()
-
-    def a_arrive(low):
-        pltpu.make_async_copy(left.at[low, core, y], left.at[low, core, y], a_recv.at[low]).wait()
-        a_onward(low)
-
-    def a_share(low):
-        view = left.at[low, core, pl.ds(0, 2)]
-        pltpu.make_async_copy(view, view, y_recv.at[low]).wait()
-        a_core(low).start()
-
-    def both_ways(step, act):
-        @pl.when(zl - step >= 0)
-        def _():
-            act(zl - step)
-
-        @pl.when(zl + step < RUN)
-        def _():
-            act(zl + step)
-
-    def b_first(half, piece, to, way):
-        return pltpu.make_async_remote_copy(
-            src_ref=own.at[half, piece], dst_ref=right.at[half, mine, x, zh],
-            send_sem=b_send.at[half, piece, way], recv_sem=b_recv.at[half, mine, zh],
-            device_id=at_z(to), device_id_type=MESH,
-        )
-
-    def b_next(half, index, high, to):
-        return pltpu.make_async_remote_copy(
-            src_ref=right.at[half, index, x, high], dst_ref=right.at[half, index, x, high],
-            send_sem=b_pass.at[half, index, high], recv_sem=b_recv.at[half, index, high],
-            device_id=at_z(to), device_id_type=MESH,
-        )
-
-    def b_side(half, index, high, step):
-        return pltpu.make_async_remote_copy(
-            src_ref=right.at[half, index, x, high], dst_ref=right.at[half, index, x, high],
-            send_sem=x_send.at[half, index, high, step - 1], recv_sem=x_recv.at[half, index],
-            device_id=at_x(step), device_id_type=MESH,
-        )
-
-    def first_of(piece):
-        gap, behind, _ = lap_of(z, piece)
-        inside = behind <= gap
-        up = jnp.where(inside, gap, 16) - behind
-        down = behind - jnp.where(inside, 0, gap)
-        return wrap(z + up, RING), up > 0, wrap(z - down + RING, RING), down > 0
-
-    wide, behind_me, far_me = lap_of(z, mine)
-    role = jnp.where(behind_me == 0, 0, 1) + jnp.where(far_me, 2, 0)
-    narrow = 16 - wide
-
-    def part(role):
-        inside = jnp.where(role < 2, 1, 2), jnp.where(role == 0, -narrow, jnp.where(role == 1, narrow, 0))
-        middle = (role == 1) | (role == 2)
-        odd = (
-            jnp.where(middle, 1, jnp.where(role == 3, 2, 3)),
-            jnp.where(role == 2, wide, jnp.where(role == 3, narrow, 0)),
-        )
-        even = (
-            jnp.where(middle, 1, jnp.where(role == 0, 2, 3)),
-            jnp.where(role == 1, -wide, jnp.where(role == 0, -narrow, 0)),
-        )
-        return [64 * hops + 32 + step for hops, step in (inside, odd, even)]
-
-    near_parts = part(role)
-    far_parts = part(wrap(role + 2, 4))
-
-    def route(index, high):
-        low = mirrored(index, high)
-        _, behind, far = lap_of(high * RUN + low, mine)
-        near_code = jnp.where(behind <= wide, near_parts[0], jnp.where(lax.rem(low + mine, 2) == 1, near_parts[1], near_parts[2]))
-        far_code = jnp.where(behind <= wide, far_parts[0], jnp.where(lax.rem(low + mine, 2) == 1, far_parts[1], far_parts[2]))
-        code = jnp.where(far, far_code, near_code)
-        step = lax.rem(code, 64) - 32
-        return lax.div(code, 64), step != 0, lax.rem(z + step + RING, RING)
-
-    def group_of(stage):
-        half = stage // RUN
-        return half, wrap(mine - (stage - half * RUN) + RUN, RUN)
-
-    def b_launch(stage):
-        half = stage // RUN
-        piece = wrap(mine + stage - half * RUN, RUN)
-        to_up, up, to_down, down = first_of(piece)
-
-        @pl.when(up)
-        def _():
-            b_first(half, piece, to_up, 1).start()
-
-        @pl.when(down)
-        def _():
-            b_first(half, piece, to_down, 0).start()
-
-    def b_handle(stage, hops_now):
-        half, index = group_of(stage)
-        for high in range(RING // RUN):
-            hops, onward, to = route(index, high)
-
-            @pl.when(hops == hops_now)
-            def _():
-                @pl.when((index != mine) | (high != zh))
-                def _():
-                    view = right.at[half, index, x, high]
-                    pltpu.make_async_copy(view, view, b_recv.at[half, index, high]).wait()
-
-                @pl.when(onward)
-                def _():
-                    b_next(half, index, high, to).start()
-
-                for side in (1, 3, 2):
-                    b_side(half, index, high, side).start()
-
-    def use(stage):
-        half, index = group_of(stage)
-        view = right.at[half, index, pl.ds(0, SIDE - 1)]
-        pltpu.make_async_copy(view, view, x_recv.at[half, index]).wait()
-        lows = [index if high % 2 == 0 else RUN - 1 - index for high in range(RING // RUN)]
-        blocks = [left[lows[high], c, high] for high in range(SIDE) for c in range(2)]
-        depths = [right[half, index, s, high] for high in range(RING // RUN) for s in range(SIDE)]
-        total[half] += jnp.dot(
-            jnp.concatenate(blocks, axis=1), jnp.concatenate(depths, axis=0), preferred_element_type=F32
-        )
-
-    def c_out(half, low):
-        return pltpu.make_async_remote_copy(
-            src_ref=done.at[half, low], dst_ref=landed.at[half, mine],
-            send_sem=c_send.at[half, low], recv_sem=c_recv.at[half],
-            device_id=device(x, y, zh * RUN + low, core), device_id_type=MESH,
-        )
-
-    def finish(half):
-        keep = (
-            lax.broadcasted_iota(jnp.int32, (tiles, HALF), 0)
-            == lax.broadcasted_iota(jnp.int32, (tiles, HALF), 1) // TILE + mine * (WIDE // TILE) + half * (HALF // TILE)
-        ).astype(F32)
-        factor = jnp.dot(c_marks[...].astype(F32), keep, preferred_element_type=F32)
-        done[half] = (total[half] * spread_rows(factor)).astype(BF16).reshape(RUN, ROWS // RUN, HALF)
-
-        @pl.loop(1, RUN)
-        def _(step):
-            c_out(half, wrap(zl + step, RUN)).start()
-
-        landed[half, mine] = done[half, zl]
-
-    a_onward(zl)
     total[...] = jnp.zeros_like(total)
     mask_copies[2].wait()
 

time: 139 us -> 139 us (level)
  no operation moved by 1% of the time
where the time goes in v4:
time: 139 us
  Pallas kernels  138 us (99%)
  local copies, waits for them, and re-layouts  1.67 us (1%)
    pallas_call x1, Pallas kernels, body(): pl.pallas_call(kernel, out_shape=jax.ShapeDtypeStruct((ROWS // RUN, width...  138 us

profile of v4, /device:TPU:1, one launch (start us, length us, event | category | flops | bytes accessed | tf_op | source)
XLA Modules:
  0.0 139.2 jit_solution(11688103524691612556)
XLA Ops:
  0.0 137.6 %purify.1 = bf16[64,2048]{1,0:T(8,128)(2,1)} custom-call(bf16[512,128]{1,0:T(8,128)(2,1)} %bitcast.7, bf16[64,2048]{1,0:T(8,128)(2,1)} %bitcast.6, s32[4,16]{1,0:T(4,128)} %bitcast.8, s32[2,64]{1,0:T(2,128)} %bitcast.9, s32[16,64]{1,0:T(8,128)} %c_mask_ref.1), custom_call_target="tpu_custom_call" | custom-call | flops 2147483648 | bytes 1048576 | tf_op jit(solution)/shard_map/purify/pallas_call | solution.py:425
  137.6 1.7 %copy.7 = bf16[64,2048]{1,0:T(8,128)(2,1)} copy(bf16[64,2048]{1,0:T(8,128)(2,1)} %purify.1) | data formatting | bytes 524288
